TPU v7x, 32 devices: a whole 2x2x4 slice. The times are simulated.
32 devices in a mesh: node: 4 (over z), space: 8 (over y, x, core).
Axes of the slice: x: 2, y: 2, z: 4, core: 2. Of those that a mesh axis runs over, the one named last changes fastest.
Arguments:
- initial: float32 [2, 64, 16, 512], P(None, 'space'), may hold values from 0 to 1
- node_guess: float32 [8, 2, 64, 16, 512], P('node', None, 'space'), may hold values from 0 to 1
- region_codes: int32 [64, 16, 512], P('space'), may hold values from 0 to 7
- coeff_table: float32 [8, 2], replicated, may hold values from 0.25 to 2
Outputs:
- node_values: float32 [8, 2, 64, 16, 512], P('node', None, 'space')
All inputs are finite; a program needn't handle non-finite values.
Results may differ from a plain program's by a relative error of at most 0.0001.
Values sent between devices are 32-bit elements; how exact they have to be, the bound alone decides.
A program may use at most 64 MiB of HBM per device.

v0:
```python
import functools
import math

import jax
import jax.numpy as jnp
import numpy as np
from jax import lax
from jax.experimental import pallas as pl
from jax.experimental.pallas import tpu as pltpu
from jax.sharding import PartitionSpec as P

SWEEPS = 2
JACOBI = 6

time_step = 1.0
feed_rate = 0.04
kill_rate = 0.06

LANES = 128


def quad_table(node_total):
    points = [
        (1.0 - math.cos(math.pi * (target + 1.0) / node_total)) / 2.0
        for target in range(node_total)
    ]
    table = []
    for target in range(node_total):
        row_values = []
        for source in range(node_total):
            coeffs = [1.0]
            for other in range(node_total):
                if other != source:
                    divisor = points[source] - points[other]
                    widened = [0.0] * (len(coeffs) + 1)
                    for power in range(len(coeffs)):
                        widened[power + 1] = widened[power + 1] + coeffs[power] / divisor
                        widened[power] = widened[power] - coeffs[power] * points[other] / divisor
                    coeffs = widened
            integral = 0.0
            for power in range(len(coeffs)):
                integral = integral + coeffs[power] * points[target] ** (power + 1) / (power + 1)
            row_values.append(integral)
        table.append(row_values)
    return (np.asarray(points, dtype=np.float32), np.asarray(table, dtype=np.float32))


def kernel(
    ring,
    spaces,
    initial_ref,
    guess_ref,
    codes_ref,
    coeff_ref,
    out_ref,
    state,
    rhs,
    gain,
    weight,
    total,
    kappa,
    packed,
    edge,
    in_send,
    in_recv,
    out_send,
    out_recv,
    kap_send,
    kap_recv,
    halo_send,
    halo_recv,
):
    mine = guess_ref.shape[0]
    nodes = mine * ring
    planes, depth = guess_ref.shape[2], guess_ref.shape[3]
    regions = coeff_ref.shape[0]
    points, quad = quad_table(nodes)
    scales = [float(np.float32(time_step) * points[m]) for m in range(nodes)]

    me = lax.axis_index("node")
    here = lax.axis_index("space")
    right = lax.rem(here + 1, spaces)
    left = lax.rem(here + spaces - 1, spaces)
    above = lax.rem(me + 1, ring)
    below = lax.rem(me + ring - 1, ring)

    def block(index):
        return pl.ds(pl.multiple_of(index * LANES, LANES), LANES)

    def remote(src, dst, send, recv, where):
        return pltpu.make_async_remote_copy(
            src_ref=src,
            dst_ref=dst,
            send_sem=send,
            recv_sem=recv,
            device_id=where,
            device_id_type=pl.DeviceIdType.MESH,
        )

    barrier = pltpu.get_barrier_semaphore()
    friends = [(lax.rem(me + step, ring), here) for step in range(1, ring)]
    friends += [(me, left), (me, right)]
    for friend in friends:
        pl.semaphore_signal(
            barrier, inc=1, device_id=friend, device_id_type=pl.DeviceIdType.MESH
        )
    pl.semaphore_wait(barrier, len(friends))

    inward = []
    for step in range(1, ring):
        target = lax.rem(me + step, ring)
        for k in range(mine):
            inward.append(
                remote(
                    guess_ref.at[k, :, :, :, block(target)],
                    state.at[0, :, me * mine + k, pl.ds(1, planes)],
                    in_send.at[step - 1, k],
                    in_recv.at[step - 1, k],
                    (target, here),
                )
            )
    for copy in inward:
        copy.start()

    row = (depth, LANES)
    lane = lax.broadcasted_iota(jnp.int32, row, 1)
    first_lane = lane == 0
    last_lane = lane == LANES - 1
    odd_lane = lax.rem(lane, 2) == 1
    pair = lane // 2
    lane_group = lane // (2 * nodes)

    def lookup(codes, f):
        found = jnp.full(row, coeff_ref[0, f], jnp.float32)
        for r in range(1, regions):
            found = jnp.where(codes == r, coeff_ref[r, f], found)
        return found

    def fill(x, carry):
        center = codes_ref[x, :, block(me)]
        before = codes_ref[x, :, block(below)]
        after = codes_ref[x, :, block(above)]
        low = jnp.where(first_lane, pltpu.roll(before, 1, 1), pltpu.roll(center, 1, 1))
        high = jnp.where(
            last_lane, pltpu.roll(after, LANES - 1, 1), pltpu.roll(center, LANES - 1, 1)
        )
        for f in range(2):
            kappa[f, x + 1] = lookup(center, f)
            weight[4, f, x] = lookup(low, f)
            weight[5, f, x] = lookup(high, f)
            for k in range(mine):
                state[0, f, me * mine + k, x + 1] = guess_ref[k, f, x, :, block(me)]
        return carry

    lax.fori_loop(0, planes, fill, 0)
    kap = [
        remote(
            kappa.at[:, 1], kappa.at[:, planes + 1], kap_send.at[0], kap_recv.at[0], (me, left)
        ),
        remote(kappa.at[:, planes], kappa.at[:, 0], kap_send.at[1], kap_recv.at[1], (me, right)),
    ]
    for copy in kap:
        copy.start()
    for copy in kap:
        copy.wait()

    def build(x, carry):
        for f in range(2):
            center = kappa[f, x + 1]
            faces = [
                (center + kappa[f, x]) * 0.5,
                (center + kappa[f, x + 2]) * 0.5,
                (center + pltpu.roll(center, 1, 0)) * 0.5,
                (center + pltpu.roll(center, depth - 1, 0)) * 0.5,
                (center + weight[4, f, x]) * 0.5,
                (center + weight[5, f, x]) * 0.5,
            ]
            summed = faces[0]
            for face in faces[1:]:
                summed = summed + face
            for side in range(6):
                weight[side, f, x] = faces[side]
            total[f, x] = summed
            for m in range(nodes):
                gain[f, m, x] = scales[m] / (1.0 + scales[m] * summed)
        return carry

    lax.fori_loop(0, planes, build, 0)

    def halo(slot, f):
        return [
            remote(
                state.at[slot, f, :, 1],
                state.at[slot, f, :, planes + 1],
                halo_send.at[slot, f, 0],
                halo_recv.at[slot, f, 0],
                (me, left),
            ),
            remote(
                state.at[slot, f, :, planes],
                state.at[slot, f, :, 0],
                halo_send.at[slot, f, 1],
                halo_recv.at[slot, f, 1],
                (me, right),
            ),
            remote(
                packed.at[slot, f],
                edge.at[slot, f, 0],
                halo_send.at[slot, f, 2],
                halo_recv.at[slot, f, 2],
                (above, here),
            ),
            remote(
                packed.at[slot, f],
                edge.at[slot, f, 1],
                halo_send.at[slot, f, 3],
                halo_recv.at[slot, f, 3],
                (below, here),
            ),
        ]

    def pack(values, slot, f, x):
        gathered = pltpu.roll(values[0], 1, 1)
        for m in range(1, nodes):
            gathered = jnp.where(pair == m, pltpu.roll(values[m], 2 * m + 1, 1), gathered)
        spread = pltpu.roll(gathered, x * (2 * nodes), 1)
        packed[slot, f] = jnp.where(lane_group == x, spread, packed[slot, f])

    def edges(slot, f):
        low = pltpu.roll(edge[slot, f, 0], 1, 1)
        high = pltpu.roll(edge[slot, f, 1], LANES - 1, 1)
        return jnp.where(odd_lane, low, high)

    def edges_at(both, x):
        return pltpu.roll(both, lax.rem((planes - x) * (2 * nodes), LANES), 1)

    def neighbours(slot, f, m, x, faces, ends):
        center = state[slot, f, m, x + 1]
        tips = pltpu.roll(ends, LANES - (2 * m + 1), 1)
        low = jnp.where(first_lane, tips, pltpu.roll(center, 1, 1))
        high = jnp.where(last_lane, tips, pltpu.roll(center, LANES - 1, 1))
        summed = faces[0] * state[slot, f, m, x] + faces[1] * state[slot, f, m, x + 2]
        summed = summed + (
            faces[2] * pltpu.roll(center, 1, 0) + faces[3] * pltpu.roll(center, depth - 1, 0)
        )
        return center, summed + (faces[4] * low + faces[5] * high)

    def opening(slot, f):
        both = edges(slot, f)

        def step(x, carry):
            faces = [weight[side, f, x] for side in range(6)]
            ends = edges_at(both, x)
            weight_total = total[f, x]
            laplaces, slopes = [], []
            for m in range(nodes):
                center, summed = neighbours(slot, f, m, x, faces, ends)
                laplace = summed - weight_total * center
                substrate = state[slot, 0, m, x + 1]
                catalyst = state[slot, 1, m, x + 1]
                product = substrate * catalyst * catalyst
                if f == 0:
                    grow = -product + feed_rate * (1.0 - substrate)
                else:
                    grow = product - (feed_rate + kill_rate) * catalyst
                laplaces.append(laplace)
                slopes.append(laplace + grow)
            start = initial_ref[f, x, :, block(me)]
            fresh = []
            for m in range(nodes):
                base = float(quad[m, 0]) * slopes[0]
                for j in range(1, nodes):
                    base = base + float(quad[m, j]) * slopes[j]
                base = start + time_step * base
                inverse = 1.0 / (1.0 + scales[m] * weight_total)
                rhs[f, m, x] = (base - scales[m] * laplaces[m]) * inverse
                center = state[slot, f, m, x + 1]
                value = (base + scales[m] * (weight_total * center)) * inverse
                state[1 - slot, f, m, x + 1] = value
                fresh.append(value)
            pack(fresh, 1 - slot, f, x)
            return carry

        lax.fori_loop(0, planes, step, 0)

    def relax(slot, f):
        both = edges(slot, f)

        def step(x, carry):
            faces = [weight[side, f, x] for side in range(6)]
            ends = edges_at(both, x)
            fresh = []
            for m in range(nodes):
                _, summed = neighbours(slot, f, m, x, faces, ends)
                value = rhs[f, m, x] + gain[f, m, x] * summed
                state[1 - slot, f, m, x + 1] = value
                fresh.append(value)
            pack(fresh, 1 - slot, f, x)
            return carry

        lax.fori_loop(0, planes, step, 0)

    def outward(f):
        copies = []
        for step in range(1, ring):
            target = lax.rem(me + step, ring)
            copies.append(
                remote(
                    state.at[0, f, pl.ds(target * mine, mine), pl.ds(1, planes)],
                    out_ref.at[:, f, :, :, block(me)],
                    out_send.at[step - 1, f],
                    out_recv.at[step - 1, f],
                    (target, here),
                )
            )
        return copies

    packed[...] = jnp.zeros(packed.shape, jnp.float32)
    for copy in inward:
        copy.wait_recv()

    for f in range(2):

        def first_pack(x, carry, f=f):
            pack([state[0, f, m, x + 1] for m in range(nodes)], 0, f, x)
            return carry

        lax.fori_loop(0, planes, first_pack, 0)
        for copy in halo(0, f):
            copy.start()

    last_step = SWEEPS * JACOBI - 1
    for sweep in range(SWEEPS):
        slot = (sweep * JACOBI) % 2
        for f in range(2):
            for copy in halo(slot, f):
                copy.wait_recv()
            if sweep > 0:
                for copy in halo(1 - slot, f):
                    copy.wait_send()
            opening(slot, f)
            for copy in halo(1 - slot, f):
                copy.start()

        def inner(t, carry, sweep=sweep):
            e = sweep * JACOBI + 1 + t // 2
            f = lax.rem(t, 2)
            slot = lax.rem(e, 2)
            for copy in halo(slot, f):
                copy.wait_recv()
            for copy in halo(1 - slot, f):
                copy.wait_send()
            relax(slot, f)
            for copy in halo(1 - slot, f):
                copy.start()
            return carry

        rounds = JACOBI - 1 if sweep < SWEEPS - 1 else JACOBI - 2
        lax.fori_loop(0, 2 * rounds, inner, 0)

    slot = last_step % 2
    for f in range(2):
        for copy in halo(slot, f):
            copy.wait_recv()
        for copy in halo(1 - slot, f):
            copy.wait_send()
        relax(slot, f)
        for copy in outward(f):
            copy.start()

        def keep(x, carry, f=f):
            for k in range(mine):
                out_ref[k, f, x, :, block(me)] = state[0, f, me * mine + k, x + 1]
            return carry

        lax.fori_loop(0, planes, keep, 0)

    for copy in inward:
        copy.wait_send()
    for f in range(2):
        for copy in halo(slot, f):
            copy.wait_send()
        for copy in outward(f):
            copy.wait()


def body(ring, spaces, initial, node_guess, region_codes, coeff_table):
    mine, fields, planes, depth, width = node_guess.shape
    nodes = mine * ring
    vmem = pltpu.VMEM
    f32 = jnp.float32
    dma = pltpu.SemaphoreType.DMA
    in_vmem = pl.BlockSpec(memory_space=pltpu.VMEM)
    return pl.pallas_call(
        functools.partial(kernel, ring, spaces),
        out_shape=jax.ShapeDtypeStruct(node_guess.shape, f32),
        in_specs=[in_vmem, in_vmem, in_vmem, pl.BlockSpec(memory_space=pltpu.SMEM)],
        out_specs=in_vmem,
        scratch_shapes=[
            vmem((2, fields, nodes, planes + 2, depth, LANES), f32),
            vmem((fields, nodes, planes, depth, LANES), f32),
            vmem((fields, nodes, planes, depth, LANES), f32),
            vmem((6, fields, planes, depth, LANES), f32),
            vmem((fields, planes, depth, LANES), f32),
            vmem((fields, planes + 2, depth, LANES), f32),
            vmem((2, fields, depth, LANES), f32),
            vmem((2, fields, 2, depth, LANES), f32),
            dma((ring - 1, mine)),
            dma((ring - 1, mine)),
            dma((ring - 1, fields)),
            dma((ring - 1, fields)),
            dma((2,)),
            dma((2,)),
            dma((2, fields, 4)),
            dma((2, fields, 4)),
        ],
        compiler_params=pltpu.CompilerParams(
            collective_id=0, has_side_effects=True, vmem_limit_bytes=32 * 1024 * 1024
        ),
    )(initial, node_guess, region_codes, coeff_table)


def solution(mesh):
    in_specs = (
        P(None, "space", None, None),
        P("node", None, "space", None, None),
        P("space", None, None),
        P(),
    )
    out_specs = P("node", None, "space", None, None)
    run = functools.partial(body, mesh.shape["node"], mesh.shape["space"])
    return jax.shard_map(run, mesh=mesh, in_specs=in_specs, out_specs=out_specs, check_vma=False)
```

profile of v0, /device:TPU:0, one launch (start us, length us, event | category | flops | bytes accessed | tf_op | source)
XLA Modules:
  0.0 197.0 jit_solution(7393906695729332503)
XLA Ops:
  0.0 0.8 copy.5.coeff_ref
  0.8 0.0 copy-start
  0.8 1.2 copy-done
  2.0 0.0 copy-start.1
  2.0 1.0 copy-done.1
  3.0 0.0 copy-start.2
  3.0 0.9 copy-done.2
  4.0 192.1 %shard_map.46 = f32[2,2,8,16,512]{4,3,2,1,0:T(8,128)S(1)} custom-call(f32[2,8,16,512]{3,2,1,0:T(8,128)S(1)} %copy-done.1, f32[2,2,8,16,512]{4,3,2,1,0:T(8,128)S(1)} %copy-done, s32[8,16,512]{2,1,0:T(8,128)S(1)} %copy-done.2, f32[8,2]{1,0:T(8,128)S(1)} %copy.5.coeff_ref), custom_call_target="tpu_custom_call" | custom-call | tf_op jit(solution)/shard_map/pallas_call | solution.py:394
  196.0 1.0 copy.7
Async XLA Ops:
  0.8 1.2 copy-start
  2.0 1.0 copy-start.1
  3.0 0.9 copy-start.2
where the time goes:
time: 197 us
  Pallas kernels  192 us (97%)
  local copies, waits for them, and re-layouts  4.94 us (3%)
    pallas_call x1, Pallas kernels, body(): pl.pallas_call(functools.partial(kernel, ring, spaces), out_shape=jax.Sha...  192 us
    unnamed x8, local copies, waits for them, and re-layouts  4.94 us

commit v1 on v0

--- a/solution.py
+++ b/solution.py
@@ -53,7 +53,8 @@
     codes_ref,
     coeff_ref,
     out_ref,
-    state,
+    state_even,
+    state_odd,
     rhs,
     gain,
     weight,
@@ -75,14 +76,22 @@
     planes, depth = guess_ref.shape[2], guess_ref.shape[3]
     regions = coeff_ref.shape[0]
     points, quad = quad_table(nodes)
+    states = (state_even, state_odd)
     scales = [float(np.float32(time_step) * points[m]) for m in range(nodes)]
 
     me = lax.axis_index("node")
     here = lax.axis_index("space")
     right = lax.rem(here + 1, spaces)
     left = lax.rem(here + spaces - 1, spaces)
-    above = lax.rem(me + 1, ring)
-    below = lax.rem(me + ring - 1, ring)
+
+    def fold(index):
+        return index + (index // 2) * (5 - 2 * index) if ring == 4 else index
+
+    own = fold(me)
+    next_block = lax.rem(own + 1, ring)
+    last_block = lax.rem(own + ring - 1, ring)
+    above = fold(next_block)
+    below = fold(last_block)
 
     def block(index):
         return pl.ds(pl.multiple_of(index * LANES, LANES), LANES)
@@ -112,8 +121,8 @@
         for k in range(mine):
             inward.append(
                 remote(
-                    guess_ref.at[k, :, :, :, block(target)],
-                    state.at[0, :, me * mine + k, pl.ds(1, planes)],
+                    guess_ref.at[k, :, :, :, block(fold(target))],
+                    state_even.at[:, me * mine + k, pl.ds(1, planes)],
                     in_send.at[step - 1, k],
                     in_recv.at[step - 1, k],
                     (target, here),
@@ -137,9 +146,9 @@
         return found
 
     def fill(x, carry):
-        center = codes_ref[x, :, block(me)]
-        before = codes_ref[x, :, block(below)]
-        after = codes_ref[x, :, block(above)]
+        center = codes_ref[x, :, block(own)]
+        before = codes_ref[x, :, block(last_block)]
+        after = codes_ref[x, :, block(next_block)]
         low = jnp.where(first_lane, pltpu.roll(before, 1, 1), pltpu.roll(center, 1, 1))
         high = jnp.where(
             last_lane, pltpu.roll(after, LANES - 1, 1), pltpu.roll(center, LANES - 1, 1)
@@ -149,7 +158,7 @@
             weight[4, f, x] = lookup(low, f)
             weight[5, f, x] = lookup(high, f)
             for k in range(mine):
-                state[0, f, me * mine + k, x + 1] = guess_ref[k, f, x, :, block(me)]
+                state_even[f, me * mine + k, x + 1] = guess_ref[k, f, x, :, block(own)]
         return carry
 
     lax.fori_loop(0, planes, fill, 0)
@@ -190,15 +199,15 @@
     def halo(slot, f):
         return [
             remote(
-                state.at[slot, f, :, 1],
-                state.at[slot, f, :, planes + 1],
+                states[slot].at[f, :, 1],
+                states[slot].at[f, :, planes + 1],
                 halo_send.at[slot, f, 0],
                 halo_recv.at[slot, f, 0],
                 (me, left),
             ),
             remote(
-                state.at[slot, f, :, planes],
-                state.at[slot, f, :, 0],
+                states[slot].at[f, :, planes],
+                states[slot].at[f, :, 0],
                 halo_send.at[slot, f, 1],
                 halo_recv.at[slot, f, 1],
                 (me, right),
@@ -219,12 +228,18 @@
             ),
         ]
 
-    def pack(values, slot, f, x):
+    def gather(values):
         gathered = pltpu.roll(values[0], 1, 1)
         for m in range(1, nodes):
             gathered = jnp.where(pair == m, pltpu.roll(values[m], 2 * m + 1, 1), gathered)
-        spread = pltpu.roll(gathered, x * (2 * nodes), 1)
-        packed[slot, f] = jnp.where(lane_group == x, spread, packed[slot, f])
+        return gathered
+
+    def pack(rows, slot, f):
+        whole = rows[0]
+        for x in range(1, planes):
+            spread = pltpu.roll(rows[x], x * (2 * nodes), 1)
+            whole = jnp.where(lane_group == x, spread, whole)
+        packed[slot, f] = whole
 
     def edges(slot, f):
         low = pltpu.roll(edge[slot, f, 0], 1, 1)
@@ -232,14 +247,15 @@
         return jnp.where(odd_lane, low, high)
 
     def edges_at(both, x):
-        return pltpu.roll(both, lax.rem((planes - x) * (2 * nodes), LANES), 1)
+        shift = ((planes - x) * (2 * nodes)) % LANES
+        return pltpu.roll(both, shift, 1) if shift else both
 
     def neighbours(slot, f, m, x, faces, ends):
-        center = state[slot, f, m, x + 1]
+        center = states[slot][f, m, x + 1]
         tips = pltpu.roll(ends, LANES - (2 * m + 1), 1)
         low = jnp.where(first_lane, tips, pltpu.roll(center, 1, 1))
         high = jnp.where(last_lane, tips, pltpu.roll(center, LANES - 1, 1))
-        summed = faces[0] * state[slot, f, m, x] + faces[1] * state[slot, f, m, x + 2]
+        summed = faces[0] * states[slot][f, m, x] + faces[1] * states[slot][f, m, x + 2]
         summed = summed + (
             faces[2] * pltpu.roll(center, 1, 0) + faces[3] * pltpu.roll(center, depth - 1, 0)
         )
@@ -247,8 +263,8 @@
 
     def opening(slot, f):
         both = edges(slot, f)
-
-        def step(x, carry):
+        rows = []
+        for x in range(planes):
             faces = [weight[side, f, x] for side in range(6)]
             ends = edges_at(both, x)
             weight_total = total[f, x]
@@ -256,8 +272,8 @@
             for m in range(nodes):
                 center, summed = neighbours(slot, f, m, x, faces, ends)
                 laplace = summed - weight_total * center
-                substrate = state[slot, 0, m, x + 1]
-                catalyst = state[slot, 1, m, x + 1]
+                substrate = states[slot][0, m, x + 1]
+                catalyst = states[slot][1, m, x + 1]
                 product = substrate * catalyst * catalyst
                 if f == 0:
                     grow = -product + feed_rate * (1.0 - substrate)
@@ -265,7 +281,7 @@
                     grow = product - (feed_rate + kill_rate) * catalyst
                 laplaces.append(laplace)
                 slopes.append(laplace + grow)
-            start = initial_ref[f, x, :, block(me)]
+            start = initial_ref[f, x, :, block(own)]
             fresh = []
             for m in range(nodes):
                 base = float(quad[m, 0]) * slopes[0]
@@ -274,31 +290,27 @@
                 base = start + time_step * base
                 inverse = 1.0 / (1.0 + scales[m] * weight_total)
                 rhs[f, m, x] = (base - scales[m] * laplaces[m]) * inverse
-                center = state[slot, f, m, x + 1]
+                center = states[slot][f, m, x + 1]
                 value = (base + scales[m] * (weight_total * center)) * inverse
-                state[1 - slot, f, m, x + 1] = value
+                states[1 - slot][f, m, x + 1] = value
                 fresh.append(value)
-            pack(fresh, 1 - slot, f, x)
-            return carry
-
-        lax.fori_loop(0, planes, step, 0)
+            rows.append(gather(fresh))
+        pack(rows, 1 - slot, f)
 
     def relax(slot, f):
         both = edges(slot, f)
-
-        def step(x, carry):
+        rows = []
+        for x in range(planes):
             faces = [weight[side, f, x] for side in range(6)]
             ends = edges_at(both, x)
             fresh = []
             for m in range(nodes):
                 _, summed = neighbours(slot, f, m, x, faces, ends)
                 value = rhs[f, m, x] + gain[f, m, x] * summed
-                state[1 - slot, f, m, x + 1] = value
+                states[1 - slot][f, m, x + 1] = value
                 fresh.append(value)
-            pack(fresh, 1 - slot, f, x)
-            return carry
-
-        lax.fori_loop(0, planes, step, 0)
+            rows.append(gather(fresh))
+        pack(rows, 1 - slot, f)
 
     def outward(f):
         copies = []
@@ -306,8 +318,8 @@
             target = lax.rem(me + step, ring)
             copies.append(
                 remote(
-                    state.at[0, f, pl.ds(target * mine, mine), pl.ds(1, planes)],
-                    out_ref.at[:, f, :, :, block(me)],
+                    state_even.at[f, pl.ds(target * mine, mine), pl.ds(1, planes)],
+                    out_ref.at[:, f, :, :, block(own)],
                     out_send.at[step - 1, f],
                     out_recv.at[step - 1, f],
                     (target, here),
@@ -315,62 +327,63 @@
             )
         return copies
 
-    packed[...] = jnp.zeros(packed.shape, jnp.float32)
     for copy in inward:
         copy.wait_recv()
 
     for f in range(2):
-
-        def first_pack(x, carry, f=f):
-            pack([state[0, f, m, x + 1] for m in range(nodes)], 0, f, x)
-            return carry
-
-        lax.fori_loop(0, planes, first_pack, 0)
+        pack(
+            [gather([state_even[f, m, x + 1] for m in range(nodes)]) for x in range(planes)], 0, f
+        )
         for copy in halo(0, f):
             copy.start()
 
-    last_step = SWEEPS * JACOBI - 1
-    for sweep in range(SWEEPS):
-        slot = (sweep * JACOBI) % 2
-        for f in range(2):
-            for copy in halo(slot, f):
-                copy.wait_recv()
-            if sweep > 0:
-                for copy in halo(1 - slot, f):
-                    copy.wait_send()
-            opening(slot, f)
-            for copy in halo(1 - slot, f):
-                copy.start()
-
-        def inner(t, carry, sweep=sweep):
-            e = sweep * JACOBI + 1 + t // 2
-            f = lax.rem(t, 2)
-            slot = lax.rem(e, 2)
-            for copy in halo(slot, f):
-                copy.wait_recv()
-            for copy in halo(1 - slot, f):
-                copy.wait_send()
-            relax(slot, f)
-            for copy in halo(1 - slot, f):
-                copy.start()
-            return carry
-
-        rounds = JACOBI - 1 if sweep < SWEEPS - 1 else JACOBI - 2
-        lax.fori_loop(0, 2 * rounds, inner, 0)
-
-    slot = last_step % 2
-    for f in range(2):
+    def advance(slot, f):
         for copy in halo(slot, f):
             copy.wait_recv()
         for copy in halo(1 - slot, f):
             copy.wait_send()
         relax(slot, f)
+
+    def send(slot, f):
+        for copy in halo(slot, f):
+            copy.start()
+
+    def both_fields(slot):
+        def one(f, carry):
+            advance(slot, f)
+            send(1 - slot, f)
+            return carry
+
+        lax.fori_loop(0, 2, one, 0)
+
+    for sweep in range(SWEEPS):
+        for f in range(2):
+            for copy in halo(0, f):
+                copy.wait_recv()
+            if sweep > 0:
+                for copy in halo(1, f):
+                    copy.wait_send()
+            opening(0, f)
+            send(1, f)
+
+        def inner(t, carry):
+            both_fields(1)
+            both_fields(0)
+            return carry
+
+        lax.fori_loop(0, (JACOBI - 2) // 2, inner, 0)
+        if sweep < SWEEPS - 1:
+            both_fields(1)
+
+    slot = 1
+    for f in range(2):
+        advance(slot, f)
         for copy in outward(f):
             copy.start()
 
         def keep(x, carry, f=f):
             for k in range(mine):
-                out_ref[k, f, x, :, block(me)] = state[0, f, me * mine + k, x + 1]
+                out_ref[k, f, x, :, block(own)] = state_even[f, me * mine + k, x + 1]
             return carry
 
         lax.fori_loop(0, planes, keep, 0)
@@ -397,7 +410,8 @@
         in_specs=[in_vmem, in_vmem, in_vmem, pl.BlockSpec(memory_space=pltpu.SMEM)],
         out_specs=in_vmem,
         scratch_shapes=[
-            vmem((2, fields, nodes, planes + 2, depth, LANES), f32),
+            vmem((fields, nodes, planes + 2, depth, LANES), f32),
+            vmem((fields, nodes, planes + 2, depth, LANES), f32),
             vmem((fields, nodes, planes, depth, LANES), f32),
             vmem((fields, nodes, planes, depth, LANES), f32),
             vmem((6, fields, planes, depth, LANES), f32),

time: 197 us -> 114 us (0.58)
  Pallas kernels: 192 us -> 109 us
    pallas_call x1, Pallas kernels: 192 us -> 109 us  [body(): pl.pallas_call(functools.partial(kernel, ring, spaces), out_shape=jax.Sha...]
where the time goes in v1:
time: 114 us
  Pallas kernels  109 us (96%)
  local copies, waits for them, and re-layouts  4.94 us (4%)
    pallas_call x1, Pallas kernels, body(): pl.pallas_call(functools.partial(kernel, ring, spaces), out_shape=jax.Sha...  109 us
    unnamed x8, local copies, waits for them, and re-layouts  4.94 us

profile of v1, /device:TPU:0, one launch (start us, length us, event | category | flops | bytes accessed | tf_op | source)
XLA Modules:
  0.0 113.8 jit_solution(1063007034776171286)
XLA Ops:
  0.0 0.8 copy.5.coeff_ref
  0.8 0.0 copy-start
  0.8 1.2 %copy-done = f32[2,2,8,16,512]{4,3,2,1,0:T(8,128)S(1)} copy-done((f32[2,2,8,16,512]{4,3,2,1,0:T(8,128)S(1)}, f32[2,2,8,16,512]{4,3,2,1,0:T(8,128)}, u32[]{:S(2)}) %copy-start) | copy-done | bytes 1048600
  2.0 0.0 copy-start.1
  2.0 1.0 copy-done.1
  3.0 0.0 copy-start.2
  3.0 0.9 copy-done.2
  4.0 108.9 %shard_map.46 = f32[2,2,8,16,512]{4,3,2,1,0:T(8,128)S(1)} custom-call(f32[2,8,16,512]{3,2,1,0:T(8,128)S(1)} %copy-done.1, f32[2,2,8,16,512]{4,3,2,1,0:T(8,128)S(1)} %copy-done, s32[8,16,512]{2,1,0:T(8,128)S(1)} %copy-done.2, f32[8,2]{1,0:T(8,128)S(1)} %copy.5.coeff_ref), custom_call_target="tpu_custom_call" | custom-call | tf_op jit(solution)/shard_map/pallas_call | solution.py:407
  112.9 1.0 copy.7
Async XLA Ops:
  0.8 1.2 %copy-start = (f32[2,2,8,16,512]{4,3,2,1,0:T(8,128)S(1)}, f32[2,2,8,16,512]{4,3,2,1,0:T(8,128)}, u32[]{:S(2)}) copy-start(f32[2,2,8,16,512]{4,3,2,1,0:T(8,128)} %guess_ref.1) | copy-start | bytes 3145732
  2.0 1.0 copy-start.1
  3.0 0.9 copy-start.2
